TPU v7x, 1024 devices: a whole 4x8x16 slice. The times are simulated.
1024 devices in a mesh: node: 128 (over z, x, y_lo), local: 8 (over y_hi, core).
Axes of the slice: x: 4, y: 8 (y_hi: 4, y_lo: 2; y = y_hi * 2 + y_lo), z: 16, core: 2. Of those that a mesh axis runs over, the one named last changes fastest.
Arguments:
- tokens: bfloat16 [2048, 4096], P('local'), may hold values from -6 to 6
- codes: bfloat16 [4096, 14336], P(('local', 'node')), may hold values from -4 to 4
- scales: bfloat16 [4096, 128], P(('local', 'node')), may hold values from 0.0078125 to 0.03125
- cotangent: bfloat16 [2048, 14336], P('local', 'node'), may hold values from -6 to 6
Outputs:
- activated: bfloat16 [2048, 14336], P('local', 'node')
- grad_weight: bfloat16 [4096, 14336], P(('local', 'node'))
All inputs are finite; a program needn't handle non-finite values.
Results may differ from a plain program's by a relative error of at most 0.0056.
Values may be sent and summed in bfloat16 or wider, within the bound.
A program may use at most 32 MiB of HBM per device.

v0:
```python
import jax
import jax.numpy as jnp
from jax import lax
from jax.sharding import PartitionSpec as P

BLK = 112


def restore(coded, block_scale):
    row_count, col_count = coded.shape
    grouped = coded.astype(jnp.float32).reshape(row_count, col_count // BLK, BLK)
    return (grouped * block_scale.astype(jnp.float32)[:, :, None]).reshape(row_count, col_count)


def body(tokens, codes, scales, cotangent):
    local_count = lax.axis_size("local")
    tok_rows = tokens.shape[0]
    col_codes, col_scales = (
        lax.all_to_all(codes, "node", split_axis=1, concat_axis=0, tiled=True),
        lax.all_to_all(scales, "node", split_axis=1, concat_axis=0, tiled=True),
    )
    piece_weight = restore(
        lax.all_gather(col_codes, "local", axis=0, tiled=True),
        lax.all_gather(col_scales, "local", axis=0, tiled=True),
    ).astype(jnp.bfloat16)
    pre = jnp.dot(tokens, piece_weight, preferred_element_type=jnp.float32)
    sig = jax.nn.sigmoid(pre)
    activated = (pre * sig).astype(jnp.bfloat16)
    grad_pre = (cotangent.astype(jnp.float32) * sig * (1.0 + pre * (1.0 - sig))).astype(
        jnp.bfloat16
    )
    factor = (tok_rows * local_count) ** (-0.5)
    partial_value = (
        lax.dot_general(
            tokens, grad_pre, (((0,), (0,)), ((), ())), preferred_element_type=jnp.float32
        )
        * factor
    )
    summed = lax.psum_scatter(partial_value, "local", scatter_dimension=0, tiled=True)
    grad_weight = lax.all_to_all(
        summed.astype(jnp.bfloat16), "node", split_axis=0, concat_axis=1, tiled=True
    )
    return (activated, grad_weight)


def solution(mesh):
    placed = (
        P("local", None),
        P(("local", "node"), None),
        P(("local", "node"), None),
        P("local", "node"),
    )
    return jax.shard_map(
        body,
        mesh=mesh,
        in_specs=placed,
        out_specs=(P("local", "node"), P(("local", "node"), None)),
        check_vma=False,
    )
```

profile of v0, /device:TPU:1, one launch (start us, length us, event | category | flops | bytes accessed | tf_op | source)
XLA Modules:
  0.0 179.6 jit_solution(458268264282768634)
XLA Ops:
  7.2 0.0 copy-start
  7.2 1.6 copy.16
  8.8 25.0 %all-to-all-start.1 = ((bf16[4,128,1]{0,2,1:T(2,128)(2,1)}), bf16[4,128,1]{0,2,1:T(2,128)(2,1)S(1)}, u32[]{:S(2)}, u32[]{:S(2)}) async-start(bf16[4,128,1]{0,2,1:T(2,128)(2,1)} %copy.16), calls=%async_computation.1 | async-start | bytes 131072 | tf_op jit(solution)/shard_map/all_to_all | solution.py:20
  33.8 1.1 all_to_all.42
  34.9 0.8 copy.15
  35.6 11.6 %all-to-all-done.1 = bf16[4,128,1]{0,2,1:T(2,128)(2,1)S(1)} async-done(((bf16[4,128,1]{0,2,1:T(2,128)(2,1)}), bf16[4,128,1]{0,2,1:T(2,128)(2,1)S(1)}, u32[]{:S(2)}, u32[]{:S(2)}) %all-to-all-start.1) | async-done | bytes 1056 | tf_op jit(solution)/shard_map/all_to_all | solution.py:20
  47.2 6.1 %all-to-all-start = ((bf16[4,128,112]{2,0,1:T(4,128)(2,1)}), bf16[4,128,112]{2,0,1:T(4,128)(2,1)S(1)}, u32[]{:S(2)}, u32[]{:S(2)}) async-start(bf16[4,128,112]{2,0,1:T(4,128)(2,1)} %copy.15), calls=%async_computation | async-start | bytes 262144 | tf_op jit(solution)/shard_map/all_to_all | solution.py:19
  53.4 0.0 reduce-scatter.2.cloned.1.call-start
  53.4 0.2 bitcast_reduce_fusion
  53.6 0.1 all_to_all.49
  53.7 17.9 %all_gather.7 = bf16[4096,1]{0,1:T(2,128)(2,1)S(1)} all-gather(bf16[512,1]{0,1:T(2,128)(2,1)S(1)} %all_to_all.49), channel_id=1, replica_groups=mesh['node'=128,'local'=8] {'local'}, dimensions={0}, use_global_device_ids=true | all-gather | bytes 9216 | tf_op jit(solution)/shard_map/all_gather | solution.py:24
  71.7 0.0 all-to-all-done
  71.7 18.3 %all_gather.6 = bf16[4096,112]{1,0:T(8,128)(2,1)S(1)} all-gather(bf16[512,112]{1,0:T(8,128)(2,1)S(1)} %bitcast.15), channel_id=1, replica_groups=mesh['node'=128,'local'=8] {'local'}, dimensions={0}, use_global_device_ids=true | all-gather | bytes 1032192 | tf_op jit(solution)/shard_map/all_gather | solution.py:23
  90.0 0.0 copy-start.1
  90.0 0.0 copy-done
  90.0 2.1 %multiply_convert_fusion.3 = (bf16[256,112]{0,1:T(8,128)(2,1)}, f32[256,112]{0,1:T(8,128)S(1)}) fusion(bf16[256,4096]{1,0:T(8,128)(2,1)S(1)} %copy-done, bf16[4096,112]{1,0:T(8,128)(2,1)S(1)} %all_gather.6, f32[4096]{0:T(1024)S(1)} %bitcast.18), kind=kOutput, calls=%fused_computation.6 | convolution fusion | flops 236400640 | bytes 3203072 | tf_op jit(solution)/shard_map/dot_general | solution.py:26
  92.1 0.0 copy-done.1
  92.1 1.8 fusion
  93.9 0.0 reduce-scatter.2.cloned.1.call-update
  93.9 45.5 %reduce-scatter.2.cloned.1.call-done = f32[512,112]{0,1:T(8,128)} async-done(((f32[4096,112]{0,1:T(8,128)}), f32[512,112]{0,1:T(8,128)}) %reduce-scatter.2.cloned.1.call-update) | async-done | bytes 229392 | tf_op jit(solution)/shard_map/reduce_scatter | solution.py:39
  139.4 1.0 convert_element_type.24
  140.4 0.1 copy.17
  140.5 31.3 %all_to_all.57 = bf16[128,4,112]{2,1,0:T(4,128)(2,1)S(1)} all-to-all(bf16[128,4,112]{2,1,0:T(4,128)(2,1)S(1)} %bitcast.16), channel_id=1, replica_groups=mesh['node'=128,'local'=8] {'node'}, dimensions={0} | all-to-all | bytes 229376 | tf_op jit(solution)/shard_map/all_to_all | solution.py:40
  171.9 0.9 all_to_all.53
  (2 shorter events, 0.0 us)
Async XLA Ops:
  7.2 82.8 %copy-start = (bf16[256,4096]{1,0:T(8,128)(2,1)S(1)}, bf16[256,4096]{1,0:T(8,128)(2,1)}, u32[]{:S(2)}) copy-start(bf16[256,4096]{1,0:T(8,128)(2,1)} %param.4) | copy-start | bytes 6291460
  8.8 38.5 %all-to-all-start.1 = ((bf16[4,128,1]{0,2,1:T(2,128)(2,1)}), bf16[4,128,1]{0,2,1:T(2,128)(2,1)S(1)}, u32[]{:S(2)}, u32[]{:S(2)}) async-start(bf16[4,128,1]{0,2,1:T(2,128)(2,1)} %copy.16), calls=%async_computation.1 | async-start | bytes 131072 | tf_op jit(solution)/shard_map/all_to_all | solution.py:20
  47.2 24.4 %all-to-all-start = ((bf16[4,128,112]{2,0,1:T(4,128)(2,1)}), bf16[4,128,112]{2,0,1:T(4,128)(2,1)S(1)}, u32[]{:S(2)}, u32[]{:S(2)}) async-start(bf16[4,128,112]{2,0,1:T(4,128)(2,1)} %copy.15), calls=%async_computation | async-start | bytes 262144 | tf_op jit(solution)/shard_map/all_to_all | solution.py:19
  53.4 86.1 %reduce-scatter.2.cloned.1.call-start = ((), (), s32[]{:S(2)}) async-start(), calls=%async_computation.4 | async-start | bytes 2064384 | tf_op jit(solution)/shard_map/reduce_scatter | solution.py:39
  90.0 2.1 %copy-start.1 = (bf16[256,112]{0,1:T(8,128)(2,1)S(1)}, bf16[256,112]{0,1:T(8,128)(2,1)}, u32[]{:S(2)}) copy-start(bf16[256,112]{0,1:T(8,128)(2,1)} %param.7) | copy-start | bytes 172036
Sparse Core Ops, SparseCore 0:
  94.0 45.3 reduce-scatter.1
where the time goes:
time: 183 us; the launch traced here: 180 us
  blocking collectives  67.5 us (37%)
  waiting for transfers between devices  57.2 us (31%)
  starting transfers between devices  31.2 us (17%)
  between operations  14.1 us (8%)
  local copies, waits for them, and re-layouts  4.82 us (3%)
  matrix products  3.91 us (2%)
    reduce_scatter x1, waiting for transfers between devices, body(): lax.psum_scatter(partial_value, 'local', scatter_dimension=0, tiled=True)  45.5 us
    all_to_all x1, blocking collectives, body(): lax.all_to_all(summed.astype(jnp.bfloat16), 'node', split_axis=0, concat_...  31.3 us
    all_to_all x1, starting transfers between devices, body(): lax.all_to_all(scales, 'node', split_axis=1, concat_axis=0, tiled=True)  25 us
    all_gather x1, blocking collectives, body(): lax.all_gather(col_codes, 'local', axis=0, tiled=True)  18.3 us
    all_gather x1, blocking collectives, body(): lax.all_gather(col_scales, 'local', axis=0, tiled=True)  17.9 us
    all_to_all x1, waiting for transfers between devices, body(): lax.all_to_all(scales, 'node', split_axis=1, concat_axis=0, tiled=True)  11.6 us
    all_to_all x1, starting transfers between devices, body(): lax.all_to_all(codes, 'node', split_axis=1, concat_axis=0, tiled=True)  6.13 us
  transfers between devices with their start and end apart: 3, of which 2 were waited for; matrix products, arithmetic and copies ran while one was open for 1% of the time, Pallas kernels for 0%

commit v1 on v0

v1 whole, which is shorter than its diff:
```python
import functools

import jax
import jax.numpy as jnp
from jax import lax
from jax.experimental import pallas as pl
from jax.experimental.pallas import tpu as pltpu
from jax.sharding import PartitionSpec as P

BLK = 112
MESH = pl.DeviceIdType.MESH
NZ, NXY, NY, NC = 16, 8, 4, 2
VMEM = pl.BlockSpec(memory_space=pltpu.VMEM)
F32, BF16 = jnp.float32, jnp.bfloat16


def kernel(
    rows, width, factor,
    tokens_hbm, codes, scales, cot_t,
    act_t, grad_out,
    tokens, wsend, wmid, wfull, pmine, psend, precv, ysend, yrecv, gblk, gmid, glast,
    tok_sem, own_sem, zs, zr, xs, xr, ys, yr, cs, cr,
    ps, pr, y2s, y2r, x2s, x2r, z2s, z2r,
):
    node, local = lax.axis_index("node"), lax.axis_index("local")
    z, xy, y, c = node // NXY, node % NXY, local // NC, local % NC
    block = NZ * NXY * rows
    partner = (node, y * NC + (1 - c))

    def at_z(other):
        return (other * NXY + xy, local)

    def at_xy(other):
        return (z * NXY + other, local)

    def at_y(other):
        return (node, other * NC + c)

    def send(src, dst, send_sem, recv_sem, device):
        copy = pltpu.make_async_remote_copy(
            src_ref=src, dst_ref=dst, send_sem=send_sem, recv_sem=recv_sem,
            device_id=device, device_id_type=MESH,
        )
        copy.start()
        return copy

    barrier = pltpu.get_barrier_semaphore()

    def greet(device):
        pl.semaphore_signal(barrier, inc=1, device_id=device, device_id_type=MESH)

    for d in range(1, NZ):
        greet(at_z((z + d) % NZ))
    for d in range(1, NXY):
        greet(at_xy((xy + d) % NXY))
    for d in range(1, NY):
        greet(at_y((y + d) % NY))
    greet(partner)

    tok_copy = pltpu.make_async_copy(tokens_hbm, tokens, tok_sem)
    tok_copy.start()

    scale = scales[...].astype(F32)
    for n in range(NZ * NXY):
        piece = codes[:, n * BLK:(n + 1) * BLK].astype(F32) * scale[:, n:n + 1]
        wsend[n // NXY, n % NXY] = piece.astype(BF16)

    pl.semaphore_wait(barrier, NZ - 1 + NXY - 1 + NY - 1 + 1)

    out = [
        send(wsend.at[(z + d) % NZ], wmid.at[z], zs.at[(z + d) % NZ], zr.at[z], at_z((z + d) % NZ))
        for d in range(1, NZ)
    ]
    own = pltpu.make_async_copy(wsend.at[z], wmid.at[z], own_sem.at[0])
    own.start()
    own.wait()
    for d in range(1, NZ):
        s = (z + d) % NZ
        pltpu.make_async_copy(wmid.at[s], wmid.at[s], zr.at[s]).wait()
    out += [
        send(wmid.at[:, (xy + d) % NXY], wfull.at[local, :, xy], xs.at[(xy + d) % NXY], xr.at[xy],
             at_xy((xy + d) % NXY))
        for d in range(1, NXY)
    ]
    own = pltpu.make_async_copy(wmid.at[:, xy], wfull.at[local, :, xy], own_sem.at[1])
    own.start()
    own.wait()
    for d in range(1, NXY):
        s = (xy + d) % NXY
        pltpu.make_async_copy(wfull.at[local, :, s], wfull.at[local, :, s], xr.at[s]).wait()

    out += [
        send(wfull.at[local], wfull.at[local], ys.at[(y + d) % NY], yr.at[y], at_y((y + d) % NY))
        for d in (2, 1, 3)
    ]
    out.append(send(wfull.at[local], wfull.at[local], cs.at[y], cr.at[y], partner))
    tok_copy.wait()

    def product(owner):
        start = pl.multiple_of(owner * block, block)
        return jnp.dot(
            tokens[:, pl.ds(start, block)], wfull[owner].reshape(block, BLK),
            preferred_element_type=F32,
        )

    pre = product(local)
    other = y * NC + 1 - c
    pltpu.make_async_copy(wfull.at[other], wfull.at[other], cr.at[y]).wait()
    pre += product(other)
    for d in (1, 3, 2):
        s = (y + d) % NY
        mine = s * NC + c
        pltpu.make_async_copy(wfull.at[mine], wfull.at[mine], yr.at[s]).wait()
        out.append(send(wfull.at[mine], wfull.at[mine], cs.at[s], cr.at[s], partner))
        pre += product(mine)
    for d in (1, 3, 2):
        s = (y + d) % NY
        other = s * NC + 1 - c
        pltpu.make_async_copy(wfull.at[other], wfull.at[other], cr.at[s]).wait()
        pre += product(other)

    sig = jax.nn.sigmoid(pre)
    act_t[...] = (pre * sig).T.astype(BF16)
    cot = cot_t[...].astype(F32).T
    grad_pre = (cot * sig * (1.0 + pre * (1.0 - sig))).astype(BF16)

    def term(owner):
        start = pl.multiple_of(owner * block, block)
        return lax.dot_general(
            tokens[:, pl.ds(start, block)], grad_pre, (((0,), (0,)), ((), ())),
            preferred_element_type=F32,
        )

    order = (2, 1, 3, 0)
    for d in order:
        s = (y + d) % NY
        psend[s] = term(s * NC + 1 - c)
        out.append(send(psend.at[s], precv.at[s], ps.at[s], pr.at[s], partner))
    for d in order:
        s = (y + d) % NY
        mine = term(s * NC + c)
        pltpu.make_async_copy(precv.at[s], precv.at[s], pr.at[s]).wait()
        mine = mine + precv[s]
        if d:
            ysend[s] = mine.astype(BF16)
            out.append(send(ysend.at[s], yrecv.at[y], y2s.at[s], y2r.at[y], at_y(s)))
        else:
            pmine[...] = mine
    total = pmine[...]
    for d in (1, 3, 2):
        s = (y + d) % NY
        pltpu.make_async_copy(yrecv.at[s], yrecv.at[s], y2r.at[s]).wait()
        total = total + yrecv[s].astype(F32)
    gblk[...] = (total * factor).astype(BF16).reshape(NZ, NXY, rows, BLK)

    out += [
        send(gblk.at[:, (xy + d) % NXY], gmid.at[:, xy], x2s.at[(xy + d) % NXY], x2r.at[xy],
             at_xy((xy + d) % NXY))
        for d in range(1, NXY)
    ]
    own = pltpu.make_async_copy(gblk.at[:, xy], gmid.at[:, xy], own_sem.at[2])
    own.start()
    own.wait()
    for d in range(1, NXY):
        s = (xy + d) % NXY
        pltpu.make_async_copy(gmid.at[:, s], gmid.at[:, s], x2r.at[s]).wait()
    out += [
        send(gmid.at[(z + d) % NZ], glast.at[z], z2s.at[(z + d) % NZ], z2r.at[z], at_z((z + d) % NZ))
        for d in range(1, NZ)
    ]
    own = pltpu.make_async_copy(gmid.at[z], glast.at[z], own_sem.at[3])
    own.start()
    own.wait()
    for d in range(1, NZ):
        s = (z + d) % NZ
        pltpu.make_async_copy(glast.at[s], glast.at[s], z2r.at[s]).wait()
    for n in range(NZ * NXY):
        grad_out[:, n * BLK:(n + 1) * BLK] = glast[n // NXY, n % NXY]
    for copy in out:
        copy.wait_send()


def body(tokens, codes, scales, cotangent):
    tok_rows, depth = tokens.shape
    rows, width = codes.shape
    block = NZ * NXY * rows
    factor = (tok_rows * NY * NC) ** (-0.5)
    piece = (NZ, NXY, rows, BLK)
    dma = pltpu.SemaphoreType.DMA
    act_t, grad = pl.pallas_call(
        functools.partial(kernel, rows, width, factor),
        out_shape=(
            jax.ShapeDtypeStruct((BLK, tok_rows), BF16),
            jax.ShapeDtypeStruct((rows, width), BF16),
        ),
        in_specs=[pl.BlockSpec(memory_space=pl.ANY), VMEM, VMEM, VMEM],
        out_specs=(VMEM, VMEM),
        scratch_shapes=[
            pltpu.VMEM((tok_rows, depth), BF16),
            pltpu.VMEM(piece, BF16),
            pltpu.VMEM(piece, BF16),
            pltpu.VMEM((NY * NC, *piece), BF16),
            pltpu.VMEM((block, BLK), F32),
            pltpu.VMEM((NY, block, BLK), F32),
            pltpu.VMEM((NY, block, BLK), F32),
            pltpu.VMEM((NY, block, BLK), BF16),
            pltpu.VMEM((NY, block, BLK), BF16),
            pltpu.VMEM(piece, BF16),
            pltpu.VMEM(piece, BF16),
            pltpu.VMEM(piece, BF16),
            dma, dma((4,)),
            dma((NZ,)), dma((NZ,)), dma((NXY,)), dma((NXY,)),
            dma((NY,)), dma((NY,)), dma((NY,)), dma((NY,)),
            dma((NY,)), dma((NY,)), dma((NY,)), dma((NY,)),
            dma((NXY,)), dma((NXY,)), dma((NZ,)), dma((NZ,)),
        ],
        compiler_params=pltpu.CompilerParams(
            collective_id=0, has_side_effects=True, vmem_limit_bytes=48 << 20
        ),
        cost_estimate=pl.CostEstimate(
            flops=4 * tok_rows * depth * BLK, bytes_accessed=4 << 20, transcendentals=tok_rows * BLK
        ),
    )(tokens, codes, scales, cotangent.T)
    return (act_t.T, grad)


def solution(mesh):
    placed = (
        P("local", None),
        P(("local", "node"), None),
        P(("local", "node"), None),
        P("local", "node"),
    )
    return jax.shard_map(
        body,
        mesh=mesh,
        in_specs=placed,
        out_specs=(P("local", "node"), P(("local", "node"), None)),
        check_vma=False,
    )
```

time: 183 us -> 88.1 us (0.48); the launches traced: 180 us -> 87.8 us
  Pallas kernels: 0 us -> 81.9 us
  blocking collectives: 67.5 us -> 0 us
  waiting for transfers between devices: 57.2 us -> 0 us
  starting transfers between devices: 31.2 us -> 0 us
  between operations: 14.1 us -> 0.65 us
  matrix products: 3.91 us -> 0 us
    pallas_call x0 -> x1, Pallas kernels: none -> 81.9 us  [body(): pl.pallas_call(functools.partial(kernel, rows, width, factor), out_shape=...]
    reduce_scatter x1 -> x0, waiting for transfers between devices: 45.5 us -> none  [body(): lax.psum_scatter(partial_value, 'local', scatter_dimension=0, tiled=True)]
    all_gather x2 -> x0, blocking collectives: 36.2 us -> none  [the longest x1 18.3 us: body(): lax.all_gather(col_codes, 'local', axis=0, tiled=True)]
    all_to_all x1 -> x0, blocking collectives: 31.3 us -> none  [body(): lax.all_to_all(summed.astype(jnp.bfloat16), 'node', split_axis=0, concat_...]
    all_to_all x2 -> x0, starting transfers between devices: 31.1 us -> none  [the longest x1 25 us: body(): lax.all_to_all(scales, 'node', split_axis=1, concat_axis=0, tiled=True)]
    all_to_all x2 -> x0, waiting for transfers between devices: 11.6 us -> none  [the longest x1 11.6 us: body(): lax.all_to_all(scales, 'node', split_axis=1, concat_axis=0, tiled=True)]
    unnamed x4 -> x10, local copies, waits for them, and re-layouts: 0.01 us -> 5.25 us
    all_to_all x7 -> x0, local copies, waits for them, and re-layouts: 4.69 us -> none  [the longest x3 1.9 us: body(): lax.all_to_all(scales, 'node', split_axis=1, concat_axis=0, tiled=True)]
  transfers between devices with their start and end apart: 3 -> 0, of which waited for: 2 -> 0; matrix products, arithmetic and copies ran while one was open for 1% -> 0% of each run, Pallas kernels for 0% -> 0%
where the time goes in v1:
time: 88.1 us; the launch traced here: 87.8 us
  Pallas kernels  81.9 us (93%)
  local copies, waits for them, and re-layouts  5.25 us (6%)
    pallas_call x1, Pallas kernels, body(): pl.pallas_call(functools.partial(kernel, rows, width, factor), out_shape=...  81.9 us
    unnamed x10, local copies, waits for them, and re-layouts  5.25 us

profile of v1, /device:TPU:1, one launch (start us, length us, event | category | flops | bytes accessed | tf_op | source)
XLA Modules:
  0.0 87.8 jit_solution(9959344221023381825)
XLA Ops:
  0.6 0.0 copy-start
  0.6 1.6 %copy-done = bf16[256,4096]{1,0:T(8,128)(2,1)S(1)} copy-done((bf16[256,4096]{1,0:T(8,128)(2,1)S(1)}, bf16[256,4096]{1,0:T(8,128)(2,1)}, u32[]{:S(2)}) %copy-start) | copy-done | bytes 2097176
  2.2 0.0 copy-start.1
  2.2 0.9 %copy-done.1 = bf16[4,14336]{1,0:T(4,128)(2,1)S(1)} copy-done((bf16[4,14336]{1,0:T(4,128)(2,1)S(1)}, bf16[4,14336]{1,0:T(4,128)(2,1)}, u32[]{:S(2)}) %copy-start.1) | copy-done | bytes 114712
  3.1 0.0 copy-start.2
  3.1 0.8 copy-done.2
  3.9 0.0 copy-start.3
  3.9 0.7 copy-done.3
  4.6 81.9 %shard_map.59 = (bf16[112,256]{1,0:T(8,128)(2,1)S(1)}, bf16[4,14336]{1,0:T(4,128)(2,1)S(1)}) custom-call(bf16[256,4096]{1,0:T(8,128)(2,1)S(1)} %copy-done, bf16[4,14336]{1,0:T(4,128)(2,1)S(1)} %copy-done.1, bf16[4,128]{1,0:T(4,128)(2,1)S(1)} %copy-done.3, bf16[112,256]{1,0:T(8,128)(2,1)S(1)} %bitcast.3), custom_call_target="tpu_custom_call" | custom-call | flops 469762048 | bytes 4194304 | tf_op jit(solution)/shard_map/pallas_call | solution.py:190
  86.5 0.6 copy.8
  87.2 0.6 copy.9
Async XLA Ops:
  0.6 1.6 %copy-start = (bf16[256,4096]{1,0:T(8,128)(2,1)S(1)}, bf16[256,4096]{1,0:T(8,128)(2,1)}, u32[]{:S(2)}) copy-start(bf16[256,4096]{1,0:T(8,128)(2,1)} %tokens_hbm.1) | copy-start | bytes 6291460
  2.2 0.9 %copy-start.1 = (bf16[4,14336]{1,0:T(4,128)(2,1)S(1)}, bf16[4,14336]{1,0:T(4,128)(2,1)}, u32[]{:S(2)}) copy-start(bf16[4,14336]{1,0:T(4,128)(2,1)} %codes.1) | copy-start | bytes 344068
  3.1 0.8 copy-start.2
  3.9 0.7 copy-start.3

commit v2 on v1

v2 whole, which is shorter than its diff:
```python
import functools

import jax
import jax.numpy as jnp
from jax import lax
from jax.experimental import pallas as pl
from jax.experimental.pallas import tpu as pltpu
from jax.sharding import PartitionSpec as P

BLK = 112
MESH = pl.DeviceIdType.MESH
NZ, NXY, NY, NC = 16, 8, 4, 2
NQ = 4
FAR_FIRST = (8, 7, 9, 6, 10, 5, 11, 4, 12, 3, 13, 2, 14, 1, 15)
VMEM = pl.BlockSpec(memory_space=pltpu.VMEM)
F32, BF16 = jnp.float32, jnp.bfloat16


def kernel(
    rows, factor,
    tokens_hbm, codes_hbm, scales_hbm, cot_hbm,
    act_t, grad_out,
    tokens, codes, scales, cot_t,
    wsend, wmid, wfull, pmine, psend, precv, ysend, yrecv, gblk, gmid, glast,
    in_sem, own_sem, zs, zr, xs, xr, ys, yr, cs, cr,
    ps, pr, y2s, y2r, x2s, x2r, z2s, z2r,
):
    node, local = lax.axis_index("node"), lax.axis_index("local")
    z, xy, y, c = node // NXY, node % NXY, local // NC, local % NC
    zq, zi = z // NQ, z % NQ
    part = NQ * NXY * rows
    block = NQ * part
    partner = (node, y * NC + (1 - c))

    def at_z(other):
        return (other * NXY + xy, local)

    def at_xy(other):
        return (z * NXY + other, local)

    def at_y(other):
        return (node, other * NC + c)

    out = []

    def send(src, dst, send_sem, recv_sem, device):
        copy = pltpu.make_async_remote_copy(
            src_ref=src, dst_ref=dst, send_sem=send_sem, recv_sem=recv_sem,
            device_id=device, device_id_type=MESH,
        )
        copy.start()
        out.append(copy)

    def landed(ref, sem):
        pltpu.make_async_copy(ref, ref, sem).wait()

    barrier = pltpu.get_barrier_semaphore()

    def greet(device):
        pl.semaphore_signal(barrier, inc=1, device_id=device, device_id_type=MESH)

    for d in FAR_FIRST:
        greet(at_z((z + d) % NZ))
    for d in range(1, NXY):
        greet(at_xy((xy + d) % NXY))
    for d in range(1, NY):
        greet(at_y((y + d) % NY))
    greet(partner)

    loads = [
        pltpu.make_async_copy(src, dst, in_sem.at[i])
        for i, (src, dst) in enumerate(
            ((codes_hbm, codes), (scales_hbm, scales), (tokens_hbm, tokens), (cot_hbm, cot_t))
        )
    ]
    for load in loads:
        load.start()
    loads[0].wait()
    loads[1].wait()

    scale = scales[...].astype(F32)
    for n in range(NZ * NXY):
        piece = codes[:, n * BLK:(n + 1) * BLK].astype(F32) * scale[:, n:n + 1]
        wsend[n // NXY, n % NXY] = piece.astype(BF16)

    pl.semaphore_wait(barrier, NZ - 1 + NXY - 1 + NY - 1 + 1)

    for d in FAR_FIRST:
        t = (z + d) % NZ
        send(wsend.at[t], wmid.at[z], zs.at[t], zr.at[z], at_z(t))
    own_z = pltpu.make_async_copy(wsend.at[z], wmid.at[z], own_sem.at[0])
    own_z.start()
    own_z.wait()

    def quarter(step):
        return (zq + step) % NQ

    def zs_of(q):
        return pl.ds(q * NQ, NQ)

    def over_xy(step):
        q = quarter(step)
        for i in range(NQ):
            if step:
                landed(wmid.at[q * NQ + i], zr.at[q * NQ + i])
            elif i:
                t = q * NQ + (zi + i) % NQ
                landed(wmid.at[t], zr.at[t])
        for d in range(1, NXY):
            t = (xy + d) % NXY
            send(wmid.at[zs_of(q), t], wfull.at[local, zs_of(q), xy], xs.at[q, t], xr.at[q, xy], at_xy(t))
        own = pltpu.make_async_copy(wmid.at[zs_of(q), xy], wfull.at[local, zs_of(q), xy], own_sem.at[1 + step])
        own.start()
        return own

    def over_y(step, own):
        q = quarter(step)
        own.wait()
        for d in range(1, NXY):
            t = (xy + d) % NXY
            landed(wfull.at[local, zs_of(q), t], xr.at[q, t])
        here = wfull.at[local, zs_of(q)]
        for d in (2, 1, 3):
            t = (y + d) % NY
            send(here, here, ys.at[q, t], yr.at[q, y], at_y(t))
        send(here, here, cs.at[q, y], cr.at[q, y], partner)

    fwd = (0, 1, 3, 2)
    last = None
    for step in fwd:
        own = over_xy(step)
        if last is not None:
            over_y(*last)
        last = (step, own)
    over_y(*last)
    loads[2].wait()
    loads[3].wait()

    def product(owner, q):
        start = pl.multiple_of(owner * block + q * part, part)
        return jnp.dot(
            tokens[:, pl.ds(start, part)], wfull[owner, zs_of(q)].reshape(part, BLK),
            preferred_element_type=F32,
        )

    pre = jnp.zeros((tokens.shape[0], BLK), F32)
    for step in fwd:
        q = quarter(step)
        for d in (1, 3, 2):
            s = (y + d) % NY
            here = wfull.at[s * NC + c, zs_of(q)]
            landed(here, yr.at[q, s])
            send(here, here, cs.at[q, s], cr.at[q, s], partner)
        for d in range(NY):
            pre += product((y + d) % NY * NC + c, q)
        for d in range(NY):
            s = (y + d) % NY
            other = s * NC + 1 - c
            landed(wfull.at[other, zs_of(q)], cr.at[q, s])
            pre += product(other, q)

    sig = jax.nn.sigmoid(pre)
    cot = cot_t[...].astype(F32).T
    grad_pre = (cot * sig * (1.0 + pre * (1.0 - sig))).astype(BF16)

    def term(owner, q):
        start = pl.multiple_of(owner * block + q * part, part)
        return lax.dot_general(
            tokens[:, pl.ds(start, part)], grad_pre, (((0,), (0,)), ((), ())),
            preferred_element_type=F32,
        )

    bwd = (2, 1, 3, 0)
    for step in bwd:
        q = quarter(step)
        for s in range(NY):
            psend[q, s] = term(s * NC + 1 - c, q)
        send(psend.at[q], precv.at[q], ps.at[q], pr.at[q], partner)
    for step in bwd:
        q = quarter(step)
        mine = [term((y + d) % NY * NC + c, q) for d in range(NY)]
        landed(precv.at[q], pr.at[q])
        for d in (2, 1, 3, 0):
            s = (y + d) % NY
            both = mine[d] + precv[q, s]
            if d:
                ysend[q, s] = both.astype(BF16)
                send(ysend.at[q, s], yrecv.at[q, y], y2s.at[q, s], y2r.at[q, y], at_y(s))
            else:
                pmine[q] = both
    act_t[...] = (pre * sig).T.astype(BF16)

    def back_xy(step):
        q = quarter(step)
        total = pmine[q]
        for d in (1, 3, 2):
            s = (y + d) % NY
            landed(yrecv.at[q, s], y2r.at[q, s])
            total = total + yrecv[q, s].astype(F32)
        gblk[zs_of(q)] = (total * factor).astype(BF16).reshape(NQ, NXY, rows, BLK)
        for d in range(1, NXY):
            t = (xy + d) % NXY
            send(gblk.at[zs_of(q), t], gmid.at[zs_of(q), xy], x2s.at[q, t], x2r.at[q, xy], at_xy(t))
        own = pltpu.make_async_copy(gblk.at[zs_of(q), xy], gmid.at[zs_of(q), xy], own_sem.at[5 + step])
        own.start()
        return own

    def back_z(step, own):
        q = quarter(step)
        own.wait()
        for d in range(1, NXY):
            s = (xy + d) % NXY
            landed(gmid.at[zs_of(q), s], x2r.at[q, s])
        for i in range(NQ):
            t = q * NQ + (i if step else (zi + i) % NQ)
            if step or i:
                send(gmid.at[t], glast.at[z], z2s.at[t], z2r.at[z], at_z(t))
        if step == 0:
            home = pltpu.make_async_copy(gmid.at[z], glast.at[z], own_sem.at[9])
            home.start()
            home.wait()

    last = None
    for step in bwd:
        own = back_xy(step)
        if last is not None:
            back_z(*last)
        last = (step, own)
    back_z(*last)
    for d in FAR_FIRST:
        s = (z + d) % NZ
        landed(glast.at[s], z2r.at[s])
    for n in range(NZ * NXY):
        grad_out[:, n * BLK:(n + 1) * BLK] = glast[n // NXY, n % NXY]
    for copy in out:
        copy.wait_send()


def body(tokens, codes, scales, cotangent):
    tok_rows, depth = tokens.shape
    rows, width = codes.shape
    part = NQ * NXY * rows
    factor = (tok_rows * NY * NC) ** (-0.5)
    piece = (NZ, NXY, rows, BLK)
    dma = pltpu.SemaphoreType.DMA
    act_t, grad = pl.pallas_call(
        functools.partial(kernel, rows, factor),
        out_shape=(
            jax.ShapeDtypeStruct((BLK, tok_rows), BF16),
            jax.ShapeDtypeStruct((rows, width), BF16),
        ),
        in_specs=[pl.BlockSpec(memory_space=pl.ANY)] * 4,
        out_specs=(VMEM, VMEM),
        scratch_shapes=[
            pltpu.VMEM((tok_rows, depth), BF16),
            pltpu.VMEM((rows, width), BF16),
            pltpu.VMEM(scales.shape, BF16),
            pltpu.VMEM((BLK, tok_rows), BF16),
            pltpu.VMEM(piece, BF16),
            pltpu.VMEM(piece, BF16),
            pltpu.VMEM((NY * NC, *piece), BF16),
            pltpu.VMEM((NQ, part, BLK), F32),
            pltpu.VMEM((NQ, NY, part, BLK), F32),
            pltpu.VMEM((NQ, NY, part, BLK), F32),
            pltpu.VMEM((NQ, NY, part, BLK), BF16),
            pltpu.VMEM((NQ, NY, part, BLK), BF16),
            pltpu.VMEM(piece, BF16),
            pltpu.VMEM(piece, BF16),
            pltpu.VMEM(piece, BF16),
            dma((4,)), dma((10,)),
            dma((NZ,)), dma((NZ,)), dma((NQ, NXY)), dma((NQ, NXY)),
            dma((NQ, NY)), dma((NQ, NY)), dma((NQ, NY)), dma((NQ, NY)),
            dma((NQ,)), dma((NQ,)), dma((NQ, NY)), dma((NQ, NY)),
            dma((NQ, NXY)), dma((NQ, NXY)), dma((NZ,)), dma((NZ,)),
        ],
        compiler_params=pltpu.CompilerParams(
            collective_id=0, has_side_effects=True, vmem_limit_bytes=62 << 20
        ),
        cost_estimate=pl.CostEstimate(
            flops=4 * tok_rows * depth * BLK, bytes_accessed=4 << 20, transcendentals=tok_rows * BLK
        ),
    )(tokens, codes, scales, cotangent.T)
    return (act_t.T, grad)


def solution(mesh):
    placed = (
        P("local", None),
        P(("local", "node"), None),
        P(("local", "node"), None),
        P("local", "node"),
    )
    return jax.shard_map(
        body,
        mesh=mesh,
        in_specs=placed,
        out_specs=(P("local", "node"), P(("local", "node"), None)),
        check_vma=False,
    )
```

time: 88.1 us -> 84.6 us (0.960)
  local copies, waits for them, and re-layouts: 5.25 us -> 3.03 us
  Pallas kernels: 81.9 us -> 80.6 us
    unnamed x10 -> x2, local copies, waits for them, and re-layouts: 5.25 us -> 3.03 us
    pallas_call x1, Pallas kernels: 81.9 us -> 80.6 us  [body(): pl.pallas_call(functools.partial(kernel, rows, factor), out_shape=(jax.Sh...]
where the time goes in v2:
time: 84.6 us; the launch traced here: 84.3 us
  Pallas kernels  80.6 us (95%)
  local copies, waits for them, and re-layouts  3.03 us (4%)
    pallas_call x1, Pallas kernels, body(): pl.pallas_call(functools.partial(kernel, rows, factor), out_shape=(jax.Sh...  80.6 us
    unnamed x2, local copies, waits for them, and re-layouts  3.03 us

profile of v2, /device:TPU:1, one launch (start us, length us, event | category | flops | bytes accessed | tf_op | source)
XLA Modules:
  0.0 84.3 jit_solution(13434460943513661286)
XLA Ops:
  0.6 80.6 %shard_map.59 = (bf16[112,256]{1,0:T(8,128)(2,1)}, bf16[4,14336]{1,0:T(4,128)(2,1)}) custom-call(bf16[256,4096]{1,0:T(8,128)(2,1)} %tokens_hbm.1, bf16[4,14336]{1,0:T(4,128)(2,1)} %codes_hbm.1, bf16[4,128]{1,0:T(4,128)(2,1)} %scales_hbm.1, bf16[112,256]{1,0:T(8,128)(2,1)} %bitcast.3), custom_call_target="tpu_custom_call" | custom-call | flops 469762048 | bytes 4194304 | tf_op jit(solution)/shard_map/pallas_call | solution.py:246
  81.3 1.4 %copy.8 = bf16[256,112]{0,1:T(8,128)(2,1)} copy(bf16[256,112]{0,1:T(8,128)(2,1)} %bitcast.2) | data formatting | bytes 114688
  82.7 1.6 %copy.9 = bf16[4,14336]{1,0:T(4,128)(2,1)} copy(bf16[4,14336]{1,0:T(4,128)(2,1)} %get-tuple-element.9) | data formatting | bytes 229376

commit v3 on v2

v3 whole, which is shorter than its diff:
```python
import functools

import jax
import jax.numpy as jnp
from jax import lax
from jax.experimental import pallas as pl
from jax.experimental.pallas import tpu as pltpu
from jax.sharding import PartitionSpec as P

BLK = 112
MESH = pl.DeviceIdType.MESH
NZ, NXY, NY, NC = 16, 8, 4, 2
NQ = 4
NEAR_FIRST = (1, 15, 2, 14, 3, 13, 4, 12, 5, 11, 6, 10, 7, 9, 8)
NEAR_QUARTERS, FAR_QUARTERS = (0, 1, 3, 2), (2, 1, 3, 0)
VMEM = pl.BlockSpec(memory_space=pltpu.VMEM)
F32, BF16 = jnp.float32, jnp.bfloat16


def kernel(
    rows, factor,
    tokens_hbm, codes_hbm, scales_hbm, cot_hbm,
    act_t, grad_out,
    tokens, codes, scales, cot_t,
    wsend, wmid, wfull, psend, precv, ysend, yrecv, gmid, glast,
    in_sem, own_sem, zs, zr, ys, yr, cs, cr,
    ps, pr, y2s, y2r, z2s, z2r,
):
    node, local = lax.axis_index("node"), lax.axis_index("local")
    z, xy, y, c = node // NXY, node % NXY, local // NC, local % NC
    zq, zi = z // NQ, z % NQ
    part = NQ * NXY * rows
    block = NQ * part
    partner = (node, y * NC + (1 - c))

    def at_z(other):
        return (other * NXY + xy, local)

    def at_plane(other_xy, other_y):
        return (z * NXY + other_xy, other_y * NC + c)

    def remote(src, dst, send_sem, recv_sem, device):
        return pltpu.make_async_remote_copy(
            src_ref=src, dst_ref=dst, send_sem=send_sem, recv_sem=recv_sem,
            device_id=device, device_id_type=MESH,
        )

    def landed(ref, sem):
        pltpu.make_async_copy(ref, ref, sem).wait()

    def plane(visit):
        for dy in (2, 1, 3, 0):
            @pl.loop(0 if dy else 1, NXY)
            def _(dx):
                visit((xy + dx) % NXY, (y + dy) % NY)

    barrier = pltpu.get_barrier_semaphore()

    def greet(device):
        pl.semaphore_signal(barrier, inc=1, device_id=device, device_id_type=MESH)

    for d in NEAR_FIRST[::-1]:
        greet(at_z((z + d) % NZ))
    plane(lambda t_xy, t_y: greet(at_plane(t_xy, t_y)))
    greet(partner)

    loads = [
        pltpu.make_async_copy(src, dst, in_sem.at[i])
        for i, (src, dst) in enumerate(
            ((codes_hbm, codes), (scales_hbm, scales), (tokens_hbm, tokens), (cot_hbm, cot_t))
        )
    ]
    for load in loads:
        load.start()
    loads[0].wait()
    loads[1].wait()

    scale = scales[...].astype(F32)
    for n in range(NZ * NXY):
        piece = codes[:, n * BLK:(n + 1) * BLK].astype(F32) * scale[:, n:n + 1]
        wsend[n // NXY, n % NXY] = piece.astype(BF16)

    pl.semaphore_wait(barrier, NZ - 1 + NXY * NY - 1 + 1)

    def z_copy(d):
        t = (z + d) % NZ
        return remote(wsend.at[t], wmid.at[z], zs.at[t], zr.at[z], at_z(t))

    for d in NEAR_FIRST:
        z_copy(d).start()
    own_z = pltpu.make_async_copy(wsend.at[z], wmid.at[z], own_sem.at[0])
    own_z.start()
    own_z.wait()

    def zs_of(q):
        return pl.ds(q * NQ, NQ)

    def plane_copy(q, t_xy, t_y):
        return remote(
            wmid.at[zs_of(q), t_xy], wfull.at[local, zs_of(q), xy],
            ys.at[q, t_y, t_xy], yr.at[q, y, xy], at_plane(t_xy, t_y),
        )

    def own_copy(step, q):
        return pltpu.make_async_copy(
            wmid.at[zs_of(q), xy], wfull.at[local, zs_of(q), xy], own_sem.at[1 + step]
        )

    for step in NEAR_QUARTERS:
        q = (zq + step) % NQ
        for i in range(NQ):
            s = q * NQ + (i if step else (zi + i) % NQ)
            if step or i:
                landed(wmid.at[s], zr.at[s])
        plane(lambda t_xy, t_y: plane_copy(q, t_xy, t_y).start())
        own_copy(step, q).start()
    loads[2].wait()
    loads[3].wait()

    def core_copy(q, s):
        here = wfull.at[s * NC + c, zs_of(q)]
        return remote(here, here, cs.at[q, s], cr.at[q, s], partner)

    def product(owner, q):
        start = pl.multiple_of(owner * block + q * part, part)
        return jnp.dot(
            tokens[:, pl.ds(start, part)], wfull[owner, zs_of(q)].reshape(part, BLK),
            preferred_element_type=F32,
        )

    pre = jnp.zeros((tokens.shape[0], BLK), F32)
    for step in NEAR_QUARTERS:
        q = (zq + step) % NQ
        for d in (0, 1, 3, 2):
            s = (y + d) % NY
            mine = s * NC + c

            @pl.loop(0 if d else 1, NXY)
            def _(dx):
                t = (xy + dx) % NXY
                landed(wfull.at[mine, zs_of(q), t], yr.at[q, s, t])

            if d == 0:
                own_copy(step, q).wait()
            core_copy(q, s).start()
            pre += product(mine, q)
        for d in (0, 1, 3, 2):
            s = (y + d) % NY
            other = s * NC + 1 - c
            landed(wfull.at[other, zs_of(q)], cr.at[q, s])
            pre += product(other, q)

    sig = jax.nn.sigmoid(pre)
    cot = cot_t[...].astype(F32).T
    grad_pre = (cot * sig * (1.0 + pre * (1.0 - sig))).astype(BF16)

    def term(owner, q):
        start = pl.multiple_of(owner * block + q * part, part)
        return lax.dot_general(
            tokens[:, pl.ds(start, part)], grad_pre, (((0,), (0,)), ((), ())),
            preferred_element_type=F32,
        )

    def pair_copy(q):
        return remote(psend.at[q], precv.at[q], ps.at[q], pr.at[q], partner)

    def back_copy(q, t_xy, t_y):
        return remote(
            ysend.at[q, t_y, :, t_xy], yrecv.at[q, y, :, xy],
            y2s.at[q, t_y, t_xy], y2r.at[q, y, xy], at_plane(t_xy, t_y),
        )

    def own_back(step, q):
        return pltpu.make_async_copy(ysend.at[q, y, :, xy], yrecv.at[q, y, :, xy], own_sem.at[5 + step])

    for step in FAR_QUARTERS:
        q = (zq + step) % NQ
        for s in range(NY):
            psend[q, s] = term(s * NC + 1 - c, q)
        pair_copy(q).start()
    for step in FAR_QUARTERS:
        q = (zq + step) % NQ
        mine = [term(s * NC + c, q) for s in range(NY)]
        landed(precv.at[q], pr.at[q])
        for s in range(NY):
            ysend[q, s] = (mine[s] + precv[q, s]).astype(BF16).reshape(NQ, NXY, rows, BLK)
        plane(lambda t_xy, t_y: back_copy(q, t_xy, t_y).start())
        own_back(step, q).start()
    act_t[...] = (pre * sig).T.astype(BF16)

    for d in NEAR_FIRST:
        z_copy(d).wait_send()
    for q in range(NQ):
        plane(lambda t_xy, t_y: plane_copy(q, t_xy, t_y).wait_send())
        for s in range(NY):
            core_copy(q, s).wait_send()
        pair_copy(q).wait_send()

    def home_copy(t):
        return remote(gmid.at[t], glast.at[z], z2s.at[t], z2r.at[z], at_z(t))

    for step in FAR_QUARTERS:
        q = (zq + step) % NQ
        own_back(step, q).wait()
        total = None
        for d in (0, 1, 3, 2):
            s = (y + d) % NY

            @pl.loop(0 if d else 1, NXY)
            def _(dx):
                t = (xy + dx) % NXY
                landed(yrecv.at[q, s, :, t], y2r.at[q, s, t])

            term_here = yrecv[q, s].reshape(part, BLK).astype(F32)
            total = term_here if total is None else total + term_here
        gmid[zs_of(q)] = (total * factor).astype(BF16).reshape(NQ, NXY, rows, BLK)
        for i in range(NQ):
            t = q * NQ + (i if step else (zi + i) % NQ)
            if step or i:
                home_copy(t).start()
    home = pltpu.make_async_copy(gmid.at[z], glast.at[z], own_sem.at[9])
    home.start()
    for q in range(NQ):
        plane(lambda t_xy, t_y: back_copy(q, t_xy, t_y).wait_send())
    home.wait()
    for d in NEAR_FIRST:
        s = (z + d) % NZ
        landed(glast.at[s], z2r.at[s])
    for n in range(NZ * NXY):
        grad_out[:, n * BLK:(n + 1) * BLK] = glast[n // NXY, n % NXY]
    for d in NEAR_FIRST:
        home_copy((z + d) % NZ).wait_send()


def body(tokens, codes, scales, cotangent):
    tok_rows, depth = tokens.shape
    rows, width = codes.shape
    part = NQ * NXY * rows
    factor = (tok_rows * NY * NC) ** (-0.5)
    piece = (NZ, NXY, rows, BLK)
    dma = pltpu.SemaphoreType.DMA
    act_t, grad = pl.pallas_call(
        functools.partial(kernel, rows, factor),
        out_shape=(
            jax.ShapeDtypeStruct((BLK, tok_rows), BF16),
            jax.ShapeDtypeStruct((rows, width), BF16),
        ),
        in_specs=[pl.BlockSpec(memory_space=pl.ANY)] * 4,
        out_specs=(VMEM, VMEM),
        scratch_shapes=[
            pltpu.VMEM((tok_rows, depth), BF16),
            pltpu.VMEM((rows, width), BF16),
            pltpu.VMEM(scales.shape, BF16),
            pltpu.VMEM((BLK, tok_rows), BF16),
            pltpu.VMEM(piece, BF16),
            pltpu.VMEM(piece, BF16),
            pltpu.VMEM((NY * NC, *piece), BF16),
            pltpu.VMEM((NQ, NY, part, BLK), F32),
            pltpu.VMEM((NQ, NY, part, BLK), F32),
            pltpu.VMEM((NQ, NY, NQ, NXY, rows, BLK), BF16),
            pltpu.VMEM((NQ, NY, NQ, NXY, rows, BLK), BF16),
            pltpu.VMEM(piece, BF16),
            pltpu.VMEM(piece, BF16),
            dma((4,)), dma((10,)), dma((NZ,)), dma((NZ,)),
            dma((NQ, NY, NXY)), dma((NQ, NY, NXY)), dma((NQ, NY)), dma((NQ, NY)),
            dma((NQ,)), dma((NQ,)), dma((NQ, NY, NXY)), dma((NQ, NY, NXY)), dma((NZ,)), dma((NZ,)),
        ],
        compiler_params=pltpu.CompilerParams(
            collective_id=0, has_side_effects=True, vmem_limit_bytes=62 << 20
        ),
        cost_estimate=pl.CostEstimate(
            flops=4 * tok_rows * depth * BLK, bytes_accessed=4 << 20, transcendentals=tok_rows * BLK
        ),
    )(tokens, codes, scales, cotangent.T)
    return (act_t.T, grad)


def solution(mesh):
    placed = (
        P("local", None),
        P(("local", "node"), None),
        P(("local", "node"), None),
        P("local", "node"),
    )
    return jax.shard_map(
        body,
        mesh=mesh,
        in_specs=placed,
        out_specs=(P("local", "node"), P(("local", "node"), None)),
        check_vma=False,
    )
```

time: 84.6 us -> 76 us (0.90)
  Pallas kernels: 80.6 us -> 72 us
    pallas_call x1, Pallas kernels: 80.6 us -> 72 us  [body(): pl.pallas_call(functools.partial(kernel, rows, factor), out_shape=(jax.Sh...]
where the time goes in v3:
time: 76 us; the launch traced here: 75.7 us
  Pallas kernels  72 us (95%)
  local copies, waits for them, and re-layouts  3.03 us (4%)
    pallas_call x1, Pallas kernels, body(): pl.pallas_call(functools.partial(kernel, rows, factor), out_shape=(jax.Sh...  72 us
    unnamed x2, local copies, waits for them, and re-layouts  3.03 us

profile of v3, /device:TPU:1, one launch (start us, length us, event | category | flops | bytes accessed | tf_op | source)
XLA Modules:
  0.0 75.7 jit_solution(1243513867350468364)
XLA Ops:
  0.6 72.0 %shard_map.59 = (bf16[112,256]{1,0:T(8,128)(2,1)}, bf16[4,14336]{1,0:T(4,128)(2,1)}) custom-call(bf16[256,4096]{1,0:T(8,128)(2,1)} %tokens_hbm.1, bf16[4,14336]{1,0:T(4,128)(2,1)} %codes_hbm.1, bf16[4,128]{1,0:T(4,128)(2,1)} %scales_hbm.1, bf16[112,256]{1,0:T(8,128)(2,1)} %bitcast.3), custom_call_target="tpu_custom_call" | custom-call | flops 469762048 | bytes 4194304 | tf_op jit(solution)/shard_map/pallas_call | solution.py:242
  72.7 1.4 %copy.8 = bf16[256,112]{0,1:T(8,128)(2,1)} copy(bf16[256,112]{0,1:T(8,128)(2,1)} %bitcast.2) | data formatting | bytes 114688
  74.1 1.6 %copy.9 = bf16[4,14336]{1,0:T(4,128)(2,1)} copy(bf16[4,14336]{1,0:T(4,128)(2,1)} %get-tuple-element.9) | data formatting | bytes 229376

commit v4 on v3

v4 whole, which is shorter than its diff:
```python
import functools

import jax
import jax.numpy as jnp
from jax import lax
from jax.experimental import pallas as pl
from jax.experimental.pallas import tpu as pltpu
from jax.sharding import PartitionSpec as P

BLK = 112
MESH = pl.DeviceIdType.MESH
NZ, NXY, NY, NC = 16, 8, 4, 2
NQ = 4
NEAR_FIRST = (1, 15, 2, 14, 3, 13, 4, 12, 5, 11, 6, 10, 7, 9, 8)
NEAR_QUARTERS, FAR_QUARTERS = (0, 1, 3, 2), (2, 1, 3, 0)
VMEM = pl.BlockSpec(memory_space=pltpu.VMEM)
F32, BF16 = jnp.float32, jnp.bfloat16


def kernel(
    rows, factor,
    tokens_hbm, codes_hbm, scales_hbm, cot_hbm,
    act_hbm, glast,
    tokens, codes, scales, cot_t, act_t,
    wsend, wmid, wfull, psend, precv, ysend, yrecv, gmid,
    in_sem, act_sem, zs, zr, ys, yr, cs, cr,
    ps, pr, y2s, y2r, z2s, z2r,
):
    node, local = lax.axis_index("node"), lax.axis_index("local")
    z, xy, y, c = node // NXY, node % NXY, local // NC, local % NC
    zq, zi = z // NQ, z % NQ
    part = NQ * NXY * rows
    block = NQ * part
    partner = (node, y * NC + (1 - c))

    def at_z(other):
        return (other * NXY + xy, local)

    def at_plane(other_xy, other_y):
        return (z * NXY + other_xy, other_y * NC + c)

    def remote(src, dst, send_sem, recv_sem, device):
        return pltpu.make_async_remote_copy(
            src_ref=src, dst_ref=dst, send_sem=send_sem, recv_sem=recv_sem,
            device_id=device, device_id_type=MESH,
        )

    def landed(ref, sem):
        pltpu.make_async_copy(ref, ref, sem).wait()

    def plane(visit):
        for dy in (2, 1, 3, 0):
            @pl.loop(0 if dy else 1, NXY)
            def _(dx):
                visit((xy + dx) % NXY, (y + dy) % NY)

    loads = [
        pltpu.make_async_copy(src, dst, in_sem.at[i])
        for i, (src, dst) in enumerate(
            ((codes_hbm, codes), (scales_hbm, scales), (tokens_hbm, tokens), (cot_hbm, cot_t))
        )
    ]
    for load in loads:
        load.start()

    barrier = pltpu.get_barrier_semaphore()

    def greet(device):
        pl.semaphore_signal(barrier, inc=1, device_id=device, device_id_type=MESH)

    for d in NEAR_FIRST[::-1]:
        greet(at_z((z + d) % NZ))
    plane(lambda t_xy, t_y: greet(at_plane(t_xy, t_y)))
    greet(partner)

    loads[0].wait()
    loads[1].wait()

    scale = scales[...].astype(F32)
    for n in range(NZ * NXY):
        piece = codes[:, n * BLK:(n + 1) * BLK].astype(F32) * scale[:, n:n + 1]
        wsend[n // NXY, n % NXY] = piece.astype(BF16)

    pl.semaphore_wait(barrier, NZ - 1 + NXY * NY - 1 + 1)

    def z_copy(d):
        t = (z + d) % NZ
        return remote(wsend.at[t], wmid.at[z], zs, zr.at[zq], at_z(t))

    for d in NEAR_FIRST:
        z_copy(d).start()
    pltpu.make_async_copy(wsend.at[z], wmid.at[z], zr.at[zq]).start()

    def zs_of(q):
        return pl.ds(q * NQ, NQ)

    def full_of(owner, q):
        return pl.ds(owner * NZ + q * NQ, NQ)

    def plane_copy(q, t_xy, t_y):
        return remote(
            wmid.at[zs_of(q), t_xy], wfull.at[full_of(local, q), xy], ys, yr.at[q, y], at_plane(t_xy, t_y)
        )

    for step in NEAR_QUARTERS:
        q = (zq + step) % NQ
        landed(wmid.at[zs_of(q)], zr.at[q])
        plane(lambda t_xy, t_y: plane_copy(q, t_xy, t_y).start())
        pltpu.make_async_copy(wmid.at[zs_of(q), xy], wfull.at[full_of(local, q), xy], yr.at[q, y]).start()
    loads[2].wait()
    loads[3].wait()

    def core_copy(q, s):
        here = wfull.at[full_of(s * NC + c, q)]
        return remote(here, here, cs, cr.at[q, s], partner)

    def product(owner, q):
        start = pl.multiple_of(owner * block + q * part, part)
        return jnp.dot(
            tokens[:, pl.ds(start, part)], wfull[full_of(owner, q)].reshape(part, BLK),
            preferred_element_type=F32,
        )

    pre = jnp.zeros((tokens.shape[0], BLK), F32)
    for step in NEAR_QUARTERS:
        q = (zq + step) % NQ
        for d in (0, 1, 3, 2):
            s = (y + d) % NY
            mine = s * NC + c
            landed(wfull.at[full_of(mine, q)], yr.at[q, s])
            core_copy(q, s).start()
            pre += product(mine, q)
        for d in (0, 1, 3, 2):
            s = (y + d) % NY
            other = s * NC + 1 - c
            landed(wfull.at[full_of(other, q)], cr.at[q, s])
            pre += product(other, q)

    sig = jax.nn.sigmoid(pre)
    cot = cot_t[...].astype(F32).T
    grad_pre = (cot * sig * (1.0 + pre * (1.0 - sig))).astype(BF16)

    def term(owner, q):
        start = pl.multiple_of(owner * block + q * part, part)
        return lax.dot_general(
            tokens[:, pl.ds(start, part)], grad_pre, (((0,), (0,)), ((), ())),
            preferred_element_type=F32,
        )

    def pair_copy(q):
        return remote(psend.at[q], precv.at[q], ps, pr.at[q], partner)

    def back_copy(q, t_xy, t_y):
        return remote(
            ysend.at[q, t_y, :, t_xy], yrecv.at[q, y, :, xy], y2s, y2r.at[q, y], at_plane(t_xy, t_y)
        )

    for step in FAR_QUARTERS:
        q = (zq + step) % NQ
        for s in range(NY):
            psend[q, s] = term(s * NC + 1 - c, q)
        pair_copy(q).start()
    for step in FAR_QUARTERS:
        q = (zq + step) % NQ
        mine = [term(s * NC + c, q) for s in range(NY)]
        landed(precv.at[q], pr.at[q])
        for s in range(NY):
            ysend[q, s] = (mine[s] + precv[q, s]).astype(BF16).reshape(NQ, NXY, rows, BLK)
        plane(lambda t_xy, t_y: back_copy(q, t_xy, t_y).start())
        pltpu.make_async_copy(ysend.at[q, y, :, xy], yrecv.at[q, y, :, xy], y2r.at[q, y]).start()
    act_t[...] = (pre * sig).T.astype(BF16)
    act_copy = pltpu.make_async_copy(act_t, act_hbm, act_sem)
    act_copy.start()

    landed(wsend.at[:NZ - 1], zs)
    landed(wfull.at[:NQ * (NXY * NY - 1) // 2], ys)
    landed(wfull.at[:NZ * NY], cs)
    landed(psend, ps)

    def home_copy(t):
        return remote(gmid.at[t], glast.at[z], z2s, z2r, at_z(t))

    for step in FAR_QUARTERS:
        q = (zq + step) % NQ
        total = None
        for d in (0, 1, 3, 2):
            s = (y + d) % NY
            landed(yrecv.at[q, s], y2r.at[q, s])
            term_here = yrecv[q, s].reshape(part, BLK).astype(F32)
            total = term_here if total is None else total + term_here
        gmid[zs_of(q)] = (total * factor).astype(BF16).reshape(NQ, NXY, rows, BLK)
        for i in range(NQ):
            t = q * NQ + (i if step else (zi + i) % NQ)
            if step or i:
                home_copy(t).start()
    pltpu.make_async_copy(gmid.at[z], glast.at[z], z2r).start()
    act_copy.wait()
    landed(wfull.at[:NQ * (NXY * NY - 1) // 2], y2s)
    landed(gmid.at[:NZ - 1], z2s)
    landed(glast, z2r)


def finish(act_in, glast, act_t, grad_out):
    act_t[...] = act_in[...]
    for n in range(NZ * NXY):
        grad_out[:, n * BLK:(n + 1) * BLK] = glast[n // NXY, n % NXY]


def body(tokens, codes, scales, cotangent):
    tok_rows, depth = tokens.shape
    rows, width = codes.shape
    part = NQ * NXY * rows
    factor = (tok_rows * NY * NC) ** (-0.5)
    piece = (NZ, NXY, rows, BLK)
    dma = pltpu.SemaphoreType.DMA
    act_t, grad = pl.pallas_call(
        functools.partial(kernel, rows, factor),
        out_shape=(
            jax.ShapeDtypeStruct((BLK, tok_rows), BF16),
            jax.ShapeDtypeStruct(piece, BF16),
        ),
        in_specs=[pl.BlockSpec(memory_space=pl.ANY)] * 4,
        out_specs=(pl.BlockSpec(memory_space=pl.ANY),) * 2,
        scratch_shapes=[
            pltpu.VMEM((tok_rows, depth), BF16),
            pltpu.VMEM((rows, width), BF16),
            pltpu.VMEM(scales.shape, BF16),
            pltpu.VMEM((BLK, tok_rows), BF16),
            pltpu.VMEM((BLK, tok_rows), BF16),
            pltpu.VMEM(piece, BF16),
            pltpu.VMEM(piece, BF16),
            pltpu.VMEM((NY * NC * NZ, NXY, rows, BLK), BF16),
            pltpu.VMEM((NQ, NY, part, BLK), F32),
            pltpu.VMEM((NQ, NY, part, BLK), F32),
            pltpu.VMEM((NQ, NY, NQ, NXY, rows, BLK), BF16),
            pltpu.VMEM((NQ, NY, NQ, NXY, rows, BLK), BF16),
            pltpu.VMEM(piece, BF16),
            dma((4,)), dma, dma, dma((NQ,)), dma, dma((NQ, NY)), dma, dma((NQ, NY)),
            dma, dma((NQ,)), dma, dma((NQ, NY)), dma, dma,
        ],
        compiler_params=pltpu.CompilerParams(
            collective_id=0, has_side_effects=True, vmem_limit_bytes=62 << 20
        ),
        cost_estimate=pl.CostEstimate(
            flops=4 * tok_rows * depth * BLK, bytes_accessed=4 << 20, transcendentals=tok_rows * BLK
        ),
    )(tokens, codes, scales, cotangent.T)
    act_t, grad = pl.pallas_call(
        finish,
        out_shape=(
            jax.ShapeDtypeStruct((BLK, tok_rows), BF16),
            jax.ShapeDtypeStruct((rows, width), BF16),
        ),
        in_specs=[VMEM, VMEM],
        out_specs=(VMEM, VMEM),
    )(act_t, grad)
    return (act_t.T, grad)


def solution(mesh):
    placed = (
        P("local", None),
        P(("local", "node"), None),
        P(("local", "node"), None),
        P("local", "node"),
    )
    return jax.shard_map(
        body,
        mesh=mesh,
        in_specs=placed,
        out_specs=(P("local", "node"), P(("local", "node"), None)),
        check_vma=False,
    )
```

time: 76 us -> 68.2 us (0.90)
  Pallas kernels: 72 us -> 67.4 us
  local copies, waits for them, and re-layouts: 3.03 us -> 0 us
    pallas_call x1, Pallas kernels: 72 us -> 65.6 us  [body(): pl.pallas_call(functools.partial(kernel, rows, factor), out_shape=(jax.Sh...]
    unnamed x2 -> x0, local copies, waits for them, and re-layouts: 3.03 us -> none
    pallas_call x0 -> x1, Pallas kernels: none -> 1.77 us  [body(): pl.pallas_call(finish, out_shape=(jax.ShapeDtypeStruct((BLK, tok_rows), B...]
where the time goes in v4:
time: 68.2 us; the launch traced here: 68 us
  Pallas kernels  67.4 us (99%)
    pallas_call x1, Pallas kernels, body(): pl.pallas_call(functools.partial(kernel, rows, factor), out_shape=(jax.Sh...  65.6 us
    pallas_call x1, Pallas kernels, body(): pl.pallas_call(finish, out_shape=(jax.ShapeDtypeStruct((BLK, tok_rows), B...  1.77 us

profile of v4, /device:TPU:1, one launch (start us, length us, event | category | flops | bytes accessed | tf_op | source)
XLA Modules:
  0.0 68.0 jit_solution(1411767203329400680)
XLA Ops:
  0.6 65.6 %shard_map.59 = (bf16[112,256]{1,0:T(8,128)(2,1)}, bf16[16,8,4,112]{3,2,1,0:T(4,128)(2,1)}) custom-call(bf16[256,4096]{1,0:T(8,128)(2,1)} %tokens_hbm.1, bf16[4,14336]{1,0:T(4,128)(2,1)} %codes_hbm.1, bf16[4,128]{1,0:T(4,128)(2,1)} %scales_hbm.1, bf16[112,256]{1,0:T(8,128)(2,1)} %bitcast.2), custom_call_target="tpu_custom_call" | custom-call | flops 469762048 | bytes 4194304 | tf_op jit(solution)/shard_map/pallas_call | solution.py:216
  66.2 1.8 %shard_map.60 = (bf16[112,256]{1,0:T(8,128)(2,1)}, bf16[4,14336]{1,0:T(4,128)(2,1)}) custom-call(bf16[112,256]{1,0:T(8,128)(2,1)} %get-tuple-element.6.act_in, bf16[16,8,4,112]{3,2,1,0:T(4,128)(2,1)} %get-tuple-element.7.glast), custom_call_target="tpu_custom_call" | custom-call | tf_op jit(solution)/shard_map/pallas_call | solution.py:248

commit v5 on v4

--- a/solution.py
+++ b/solution.py
@@ -12,7 +12,8 @@
 NZ, NXY, NY, NC = 16, 8, 4, 2
 NQ = 4
 NEAR_FIRST = (1, 15, 2, 14, 3, 13, 4, 12, 5, 11, 6, 10, 7, 9, 8)
-NEAR_QUARTERS, FAR_QUARTERS = (0, 1, 3, 2), (2, 1, 3, 0)
+NEAR_QUARTERS = (0, 1, 3, 2)
+BACK_QUARTERS = (0, 1, 2, 3)
 VMEM = pl.BlockSpec(memory_space=pltpu.VMEM)
 F32, BF16 = jnp.float32, jnp.bfloat16
 
@@ -28,7 +29,7 @@
 ):
     node, local = lax.axis_index("node"), lax.axis_index("local")
     z, xy, y, c = node // NXY, node % NXY, local // NC, local % NC
-    zq, zi = z // NQ, z % NQ
+    zq = z // NQ
     part = NQ * NXY * rows
     block = NQ * part
     partner = (node, y * NC + (1 - c))
@@ -99,14 +100,14 @@
 
     def plane_copy(q, t_xy, t_y):
         return remote(
-            wmid.at[zs_of(q), t_xy], wfull.at[full_of(local, q), xy], ys, yr.at[q, y], at_plane(t_xy, t_y)
+            wmid.at[zs_of(q), t_xy], wfull.at[full_of(local, q), xy], ys, yr.at[q], at_plane(t_xy, t_y)
         )
 
     for step in NEAR_QUARTERS:
         q = (zq + step) % NQ
         landed(wmid.at[zs_of(q)], zr.at[q])
         plane(lambda t_xy, t_y: plane_copy(q, t_xy, t_y).start())
-        pltpu.make_async_copy(wmid.at[zs_of(q), xy], wfull.at[full_of(local, q), xy], yr.at[q, y]).start()
+        pltpu.make_async_copy(wmid.at[zs_of(q), xy], wfull.at[full_of(local, q), xy], yr.at[q]).start()
     loads[2].wait()
     loads[3].wait()
 
@@ -124,11 +125,12 @@
     pre = jnp.zeros((tokens.shape[0], BLK), F32)
     for step in NEAR_QUARTERS:
         q = (zq + step) % NQ
+        landed(wfull.at[:NZ], yr.at[q])
+        for d in range(NY):
+            core_copy(q, d).start()
         for d in (0, 1, 3, 2):
             s = (y + d) % NY
             mine = s * NC + c
-            landed(wfull.at[full_of(mine, q)], yr.at[q, s])
-            core_copy(q, s).start()
             pre += product(mine, q)
         for d in (0, 1, 3, 2):
             s = (y + d) % NY
@@ -152,22 +154,30 @@
 
     def back_copy(q, t_xy, t_y):
         return remote(
-            ysend.at[q, t_y, :, t_xy], yrecv.at[q, y, :, xy], y2s, y2r.at[q, y], at_plane(t_xy, t_y)
-        )
-
-    for step in FAR_QUARTERS:
-        q = (zq + step) % NQ
+            ysend.at[q, t_y, :, t_xy], yrecv.at[q, y, :, xy], y2s, y2r.at[q], at_plane(t_xy, t_y)
+        )
+
+    def to_pair(q):
         for s in range(NY):
             psend[q, s] = term(s * NC + 1 - c, q)
         pair_copy(q).start()
-    for step in FAR_QUARTERS:
-        q = (zq + step) % NQ
+
+    def to_plane(q):
         mine = [term(s * NC + c, q) for s in range(NY)]
         landed(precv.at[q], pr.at[q])
         for s in range(NY):
             ysend[q, s] = (mine[s] + precv[q, s]).astype(BF16).reshape(NQ, NXY, rows, BLK)
         plane(lambda t_xy, t_y: back_copy(q, t_xy, t_y).start())
-        pltpu.make_async_copy(ysend.at[q, y, :, xy], yrecv.at[q, y, :, xy], y2r.at[q, y]).start()
+        pltpu.make_async_copy(ysend.at[q, y, :, xy], yrecv.at[q, y, :, xy], y2r.at[q]).start()
+
+    to_pair(BACK_QUARTERS[0])
+    to_pair(BACK_QUARTERS[1])
+    to_plane(BACK_QUARTERS[0])
+    to_pair(BACK_QUARTERS[2])
+    to_plane(BACK_QUARTERS[1])
+    to_pair(BACK_QUARTERS[3])
+    to_plane(BACK_QUARTERS[2])
+    to_plane(BACK_QUARTERS[3])
     act_t[...] = (pre * sig).T.astype(BF16)
     act_copy = pltpu.make_async_copy(act_t, act_hbm, act_sem)
     act_copy.start()
@@ -180,19 +190,21 @@
     def home_copy(t):
         return remote(gmid.at[t], glast.at[z], z2s, z2r, at_z(t))
 
-    for step in FAR_QUARTERS:
-        q = (zq + step) % NQ
+    for q in BACK_QUARTERS:
+        landed(yrecv.at[q], y2r.at[q])
         total = None
         for d in (0, 1, 3, 2):
             s = (y + d) % NY
-            landed(yrecv.at[q, s], y2r.at[q, s])
             term_here = yrecv[q, s].reshape(part, BLK).astype(F32)
             total = term_here if total is None else total + term_here
         gmid[zs_of(q)] = (total * factor).astype(BF16).reshape(NQ, NXY, rows, BLK)
         for i in range(NQ):
-            t = q * NQ + (i if step else (zi + i) % NQ)
-            if step or i:
+            t = q * NQ + i
+
+            @pl.when(t != z)
+            def _():
                 home_copy(t).start()
+
     pltpu.make_async_copy(gmid.at[z], glast.at[z], z2r).start()
     act_copy.wait()
     landed(wfull.at[:NQ * (NXY * NY - 1) // 2], y2s)
@@ -235,8 +247,8 @@
             pltpu.VMEM((NQ, NY, NQ, NXY, rows, BLK), BF16),
             pltpu.VMEM((NQ, NY, NQ, NXY, rows, BLK), BF16),
             pltpu.VMEM(piece, BF16),
-            dma((4,)), dma, dma, dma((NQ,)), dma, dma((NQ, NY)), dma, dma((NQ, NY)),
-            dma, dma((NQ,)), dma, dma((NQ, NY)), dma, dma,
+            dma((4,)), dma, dma, dma((NQ,)), dma, dma((NQ,)), dma, dma((NQ, NY)),
+            dma, dma((NQ,)), dma, dma((NQ,)), dma, dma,
         ],
         compiler_params=pltpu.CompilerParams(
             collective_id=0, has_side_effects=True, vmem_limit_bytes=62 << 20

time: 68.2 us -> 68.2 us (level)
  no operation moved by 1% of the time
where the time goes in v5:
time: 68.2 us; the launch traced here: 68 us
  Pallas kernels  67.3 us (99%)
    pallas_call x1, Pallas kernels, body(): pl.pallas_call(functools.partial(kernel, rows, factor), out_shape=(jax.Sh...  65.6 us
    pallas_call x1, Pallas kernels, body(): pl.pallas_call(finish, out_shape=(jax.ShapeDtypeStruct((BLK, tok_rows), B...  1.77 us

profile of v5, /device:TPU:1, one launch (start us, length us, event | category | flops | bytes accessed | tf_op | source)
XLA Modules:
  0.0 68.0 jit_solution(5374415992167720573)
XLA Ops:
  0.6 65.6 %shard_map.59 = (bf16[112,256]{1,0:T(8,128)(2,1)}, bf16[16,8,4,112]{3,2,1,0:T(4,128)(2,1)}) custom-call(bf16[256,4096]{1,0:T(8,128)(2,1)} %tokens_hbm.1, bf16[4,14336]{1,0:T(4,128)(2,1)} %codes_hbm.1, bf16[4,128]{1,0:T(4,128)(2,1)} %scales_hbm.1, bf16[112,256]{1,0:T(8,128)(2,1)} %bitcast.2), custom_call_target="tpu_custom_call" | custom-call | flops 469762048 | bytes 4194304 | tf_op jit(solution)/shard_map/pallas_call | solution.py:228
  66.2 1.8 %shard_map.60 = (bf16[112,256]{1,0:T(8,128)(2,1)}, bf16[4,14336]{1,0:T(4,128)(2,1)}) custom-call(bf16[112,256]{1,0:T(8,128)(2,1)} %get-tuple-element.6.act_in, bf16[16,8,4,112]{3,2,1,0:T(4,128)(2,1)} %get-tuple-element.7.glast), custom_call_target="tpu_custom_call" | custom-call | tf_op jit(solution)/shard_map/pallas_call | solution.py:260
